TPU v7x, 32 devices: a whole 2x2x4 slice. The times are simulated.
32 devices in a mesh: pipe: 2 (over x), seq: 4 (over y, core), fsdp: 4 (over z).
Axes of the slice: x: 2, y: 2, z: 4, core: 2. Of those that a mesh axis runs over, the one named last changes fastest.
Arguments:
- embedded: bfloat16 [512, 2688], P('seq', 'fsdp'), may hold values from -6 to 6
- sent_forward: bfloat16 [2, 512, 2688], P('pipe', 'seq', 'fsdp'), may hold values from -6 to 6
- stashed: bfloat16 [2, 512, 2688], P('pipe', 'seq', 'fsdp'), may hold values from -6 to 6
- sent_backward: bfloat16 [2, 512, 2688], P('pipe', 'seq', 'fsdp'), may hold values from -6 to 6
- loss_grad: bfloat16 [512, 2688], P('seq', 'fsdp'), may hold values from -6 to 6
- norm_gain: float32 [2, 2688], P('pipe'), may hold values from 0.5 to 2
- w_query: bfloat16 [2, 2688, 2048], P('pipe', None, 'fsdp'), may hold values from -1 to 1
- w_key: bfloat16 [2, 2688, 1024], P('pipe', None, 'fsdp'), may hold values from -1 to 1
- value_projection: bfloat16 [2, 2688, 1024], P('pipe', None, 'fsdp'), may hold values from -0.125 to 0.125
- w_out: bfloat16 [2, 2048, 2688], P('pipe', 'fsdp'), may hold values from -0.125 to 0.125
- forward_docs: int32 [2, 512], P('pipe'), may hold values from 0 to 3, never falling along the last dimension, each value on 1 to 256 neighbouring positions
- backward_docs: int32 [2, 512], P('pipe'), may hold values from 0 to 3, never falling along the last dimension, each value on 1 to 256 neighbouring positions
Outputs:
- forward_out: bfloat16 [2, 512, 2688], P('pipe', 'seq', 'fsdp')
- input_grad: bfloat16 [2, 512, 2688], P('pipe', 'seq', 'fsdp')
Inputs may be any that keep to these rules, and one draw needn't show every extreme that they name: `forward_docs`: document numbers never fall along a sequence; every document is a run of 1 to 256 tokens. `backward_docs`: document numbers never fall along a sequence; every document is a run of 1 to 256 tokens.
All inputs are finite; a program needn't handle non-finite values.
Results may differ from a plain program's by a relative error of at most 0.015.
Values may be sent and summed in bfloat16 or wider, within the bound.
A program may use at most 64 MiB of HBM per device.

v0:
```python
import jax
import jax.numpy as jnp
from jax import lax
from jax.sharding import PartitionSpec as P

MODEL_WIDTH = 2688
QUERY_HEADS = 16
KEY_VALUE_HEADS = 8
HEAD_SIZE = 128
WINDOW_TOKENS = 512


def from_behind(value, axis, steps):
    count = lax.axis_size(axis)
    initial, last = (max(0, -steps), min(count, count - steps))
    return lax.ppermute(value, axis, [(source, source + steps) for source in range(initial, last)])


def normalize(rows_in, gain):
    value_rows = rows_in.astype(jnp.float32)
    row_scale_factor = lax.rsqrt(jnp.mean(value_rows * value_rows, axis=-1, keepdims=True) + 1e-06)
    return ((value_rows * row_scale_factor * gain).astype(jnp.bfloat16), row_scale_factor)


def block_probs(query_block, k_block, q_pos, k_pos, q_doc, k_doc):
    scores = jnp.einsum("qhgd,khd->hgqk", query_block, k_block, preferred_element_type=jnp.float32)
    scores = scores * HEAD_SIZE ** (-0.5)
    keep = (k_pos[None, :] <= q_pos[:, None]) & (q_pos[:, None] - k_pos[None, :] < WINDOW_TOKENS)
    keep = keep & (k_doc[None, :] == q_doc[:, None])
    scores = jnp.where(keep, scores, -1e30)
    top = jnp.max(scores, axis=-1, keepdims=True)
    expo = jnp.exp(scores - top)
    return expo / jnp.sum(expo, axis=-1, keepdims=True)


def near_rows(both, hops):
    pieces = [from_behind(both, "seq", distance) for distance in range(hops, 0, -1)]
    return jnp.concatenate(pieces + [both], 0)


def return_terms(terms, hops, length):
    total = jnp.zeros((length, terms.shape[1]), jnp.float32)
    for distance in range(1, hops + 1):
        piece = terms[(hops - distance) * length : (hops - distance + 1) * length]
        total = total + from_behind(piece.astype(jnp.bfloat16), "seq", -distance).astype(
            piece.dtype
        )
    return total


def contract_last(left, right):
    return lax.dot_general(
        left, right, (((1,), (1,)), ((), ())), preferred_element_type=jnp.float32
    )


def per_device(
    embedded,
    sent_forward,
    stashed,
    sent_backward,
    loss_grad,
    norm_gain,
    w_query,
    w_key,
    value_projection,
    w_out,
    forward_docs,
    backward_docs,
):
    length = embedded.shape[0]
    share = embedded.shape[1]
    section = lax.axis_index("pipe")
    sections = lax.axis_size("pipe")
    arrived = from_behind(sent_forward[0], "pipe", 1)
    incoming = jnp.where(section == 0, embedded, arrived)
    returned = from_behind(sent_backward[0], "pipe", -1)
    upstream = jnp.where(section == sections - 1, loss_grad, returned)
    x_full, stash_full, upstream_full = (
        lax.all_gather(incoming, "fsdp", axis=1, tiled=True),
        lax.all_gather(stashed[0], "fsdp", axis=1, tiled=True),
        lax.all_gather(upstream, "fsdp", axis=1, tiled=True),
    )
    gain = norm_gain[0]
    query_weight, key_weight, value_weight, out_weight = (
        w_query[0],
        w_key[0],
        value_projection[0],
        w_out[0],
    )
    h_forward, scale_forward = normalize(x_full, gain)
    h_backward, scale_backward = normalize(stash_full, gain)
    stacked = jnp.concatenate([h_forward, h_backward], 0)
    query_rows = jnp.dot(stacked, query_weight, preferred_element_type=jnp.float32).astype(
        jnp.bfloat16
    )
    key_rows = jnp.dot(stacked, key_weight, preferred_element_type=jnp.float32).astype(jnp.bfloat16)
    value_rows = jnp.dot(stacked, value_weight, preferred_element_type=jnp.float32).astype(
        jnp.bfloat16
    )
    key_cols = key_rows.shape[1]
    kv_heads = key_cols // HEAD_SIZE
    head_groups = QUERY_HEADS // KEY_VALUE_HEADS
    both = jnp.concatenate(
        [key_rows[:length], value_rows[:length], key_rows[length:], value_rows[length:]], 1
    )
    hops = min(WINDOW_TOKENS // length, lax.axis_size("seq") - 1)
    window_rows = near_rows(both, hops)
    span = (hops + 1) * length
    query_start = lax.axis_index("seq") * length
    q_pos = query_start + jnp.arange(length, dtype=jnp.int32)
    k_pos = query_start - hops * length + jnp.arange(span, dtype=jnp.int32)
    pad_ids = jnp.full((WINDOW_TOKENS,), -1, jnp.int32)
    docs_fwd = jnp.concatenate([pad_ids, forward_docs[0]])
    docs_bwd = jnp.concatenate([pad_ids, backward_docs[0]])
    k_start = query_start - hops * length + WINDOW_TOKENS
    q_fwd = query_rows[:length].reshape(length, kv_heads, head_groups, HEAD_SIZE)
    k_fwd = window_rows[:, :key_cols].reshape(span, kv_heads, HEAD_SIZE)
    v_fwd = window_rows[:, key_cols : 2 * key_cols].reshape(span, kv_heads, HEAD_SIZE)
    probs_fwd = block_probs(
        q_fwd,
        k_fwd,
        q_pos,
        k_pos,
        lax.dynamic_slice_in_dim(docs_fwd, query_start + WINDOW_TOKENS, length, 0),
        lax.dynamic_slice_in_dim(docs_fwd, k_start, span, 0),
    ).astype(jnp.bfloat16)
    attn_fwd = (
        jnp.einsum("hgqk,khd->qhgd", probs_fwd, v_fwd, preferred_element_type=jnp.float32)
        .reshape(length, -1)
        .astype(jnp.bfloat16)
    )
    partial_out = jnp.dot(attn_fwd, out_weight, preferred_element_type=jnp.float32)
    summed = lax.psum_scatter(
        partial_out.astype(jnp.bfloat16), "fsdp", scatter_dimension=1, tiled=True
    ).astype(jnp.float32)
    forward_out = (incoming.astype(jnp.float32) + summed).astype(jnp.bfloat16)
    q_bwd = query_rows[length:].reshape(length, kv_heads, head_groups, HEAD_SIZE)
    k_bwd = window_rows[:, 2 * key_cols : 3 * key_cols].reshape(span, kv_heads, HEAD_SIZE)
    v_bwd = window_rows[:, 3 * key_cols :].reshape(span, kv_heads, HEAD_SIZE)
    probs = block_probs(
        q_bwd,
        k_bwd,
        q_pos,
        k_pos,
        lax.dynamic_slice_in_dim(docs_bwd, query_start + WINDOW_TOKENS, length, 0),
        lax.dynamic_slice_in_dim(docs_bwd, k_start, span, 0),
    )
    probs_low = probs.astype(jnp.bfloat16)
    attention_gradient = (
        contract_last(upstream_full, out_weight)
        .astype(jnp.bfloat16)
        .reshape(length, kv_heads, head_groups, HEAD_SIZE)
    )
    dv_terms = jnp.einsum(
        "hgqk,qhgd->khd", probs_low, attention_gradient, preferred_element_type=jnp.float32
    )
    dp_block = jnp.einsum(
        "qhgd,khd->hgqk", attention_gradient, v_bwd, preferred_element_type=jnp.float32
    )
    delta = jnp.sum(probs * dp_block, axis=-1, keepdims=True)
    ds_block = (probs * (dp_block - delta)).astype(jnp.bfloat16)
    dq_local = (
        (
            jnp.einsum("hgqk,khd->qhgd", ds_block, k_bwd, preferred_element_type=jnp.float32)
            * HEAD_SIZE ** (-0.5)
        )
        .reshape(length, -1)
        .astype(jnp.bfloat16)
    )
    dk_terms = jnp.einsum(
        "hgqk,qhgd->khd", ds_block, q_bwd, preferred_element_type=jnp.float32
    ) * HEAD_SIZE ** (-0.5)
    kv_terms = jnp.concatenate(
        [dk_terms.reshape(span, key_cols), dv_terms.reshape(span, key_cols)], 1
    )
    owned = kv_terms[hops * length :] + return_terms(kv_terms, hops, length)
    dk_local = owned[:, :key_cols].astype(jnp.bfloat16)
    dv_local = owned[:, key_cols:].astype(jnp.bfloat16)
    d_norm = (
        contract_last(dq_local, query_weight)
        + contract_last(dk_local, key_weight)
        + contract_last(dv_local, value_weight)
    )
    feature_start = lax.axis_index("fsdp") * share
    d_share = lax.psum_scatter(
        d_norm.astype(jnp.bfloat16), "fsdp", scatter_dimension=1, tiled=True
    ).astype(jnp.float32)
    gain_share = lax.dynamic_slice_in_dim(gain, feature_start, share, 0)
    values_own = stashed[0].astype(jnp.float32)
    row_part = jnp.sum(values_own * gain_share * d_share, axis=-1, keepdims=True)
    row_mean = lax.psum(row_part, "fsdp") / MODEL_WIDTH
    d_input = scale_backward * gain_share * d_share - values_own * scale_backward**3 * row_mean
    input_grad = (upstream.astype(jnp.float32) + d_input).astype(jnp.bfloat16)
    return (forward_out[None], input_grad[None])


def solution(mesh):
    placed = (
        P("seq", "fsdp"),
        P("pipe", "seq", "fsdp"),
        P("pipe", "seq", "fsdp"),
        P("pipe", "seq", "fsdp"),
        P("seq", "fsdp"),
        P("pipe", None),
        P("pipe", None, "fsdp"),
        P("pipe", None, "fsdp"),
        P("pipe", None, "fsdp"),
        P("pipe", "fsdp", None),
        P("pipe", None),
        P("pipe", None),
    )
    return jax.shard_map(
        per_device,
        mesh=mesh,
        in_specs=placed,
        out_specs=(P("pipe", "seq", "fsdp"), P("pipe", "seq", "fsdp")),
        check_vma=False,
    )
```

profile of v0, /device:TPU:0, one launch (start us, length us, event | category | flops | bytes accessed | tf_op | source)
XLA Modules:
  0.0 169.2 jit_solution(25202959076852527)
XLA Ops:
  7.3 5.8 %collective-permute-start = (bf16[128,672]{0,1:T(8,128)(2,1)}, bf16[128,672]{0,1:T(8,128)(2,1)}, u32[]{:S(2)}, u32[]{:S(2)}) collective-permute-start(bf16[128,672]{0,1:T(8,128)(2,1)} %bitcast.157), channel_id=1, source_target_pairs={{0,16},{1,17},{2,18},{3,19},{4,20},{5,21},{6,22},{7,23},{8,24},{9,... | collective-permute-start | bytes 516104 | tf_op jit(solution)/shard_map/ppermute | solution.py:16
  14.3 18.8 %all-gather = bf16[1,128,2688]{1,2,0:T(8,128)(2,1)S(1)} all-gather(bf16[1,128,672]{1,2,0:T(8,128)(2,1)} %param.14), channel_id=2, replica_groups=mesh['pipe'=2,'seq'=4,'fsdp'=4] {'fsdp'}, dimensions={2}, use_global_device_ids=true | all-gather | bytes 860160 | tf_op jit(solution)/shard_map/all_gather | solution.py:81
  37.4 16.3 %all_gather.9 = bf16[128,2688]{0,1:T(8,128)(2,1)S(1)} all-gather(bf16[128,672]{0,1:T(8,128)(2,1)S(1)} %broadcast_select_fusion.1), channel_id=1, replica_groups=mesh['pipe'=2,'seq'=4,'fsdp'=4] {'fsdp'}, dimensions={1}, use_global_device_ids=true | all-gather | bytes 860160 | tf_op jit(solution)/shard_map/all_gather | solution.py:80
  58.2 2.0 %collective-permute-start.3 = (bf16[128,1024]{0,1:T(8,128)(2,1)}, bf16[128,1024]{0,1:T(8,128)(2,1)}, u32[]{:S(2)}, u32[]{:S(2)}) collective-permute-start(bf16[128,1024]{0,1:T(8,128)(2,1)} %pad_maximum_fusion.5), channel_id=1, source_target_pairs={{0,4},{4,8},{8,12},{1,5},{5,9},{9,13},{2,6},{6,10},{10,14},{3,7},{... | collective-permute-start | bytes 786440 | tf_op jit(solution)/shard_map/ppermute | solution.py:16
  60.2 4.1 %collective-permute-start.2 = (bf16[128,1024]{0,1:T(8,128)(2,1)}, bf16[128,1024]{0,1:T(8,128)(2,1)}, u32[]{:S(2)}, u32[]{:S(2)}) collective-permute-start(bf16[128,1024]{0,1:T(8,128)(2,1)} %pad_maximum_fusion.5), channel_id=1, source_target_pairs={{0,8},{4,12},{1,9},{5,13},{2,10},{6,14},{3,11},{7,15},{16,24},{20,... | collective-permute-start | bytes 786440 | tf_op jit(solution)/shard_map/ppermute | solution.py:16
  64.3 2.0 %collective-permute-start.1 = (bf16[128,1024]{0,1:T(8,128)(2,1)}, bf16[128,1024]{0,1:T(8,128)(2,1)}, u32[]{:S(2)}, u32[]{:S(2)}) collective-permute-start(bf16[128,1024]{0,1:T(8,128)(2,1)} %pad_maximum_fusion.5), channel_id=1, source_target_pairs={{0,12},{1,13},{2,14},{3,15},{16,28},{17,29},{18,30},{19,31}} | collective-permute-start | bytes 786440 | tf_op jit(solution)/shard_map/ppermute | solution.py:16
  69.6 16.7 %all_gather.11 = bf16[128,2688]{0,1:T(8,128)(2,1)S(1)} all-gather(bf16[128,672]{0,1:T(8,128)(2,1)S(1)} %broadcast_select_fusion), channel_id=1, replica_groups=mesh['pipe'=2,'seq'=4,'fsdp'=4] {'fsdp'}, dimensions={1}, use_global_device_ids=true | all-gather | bytes 860160 | tf_op jit(solution)/shard_map/all_gather | solution.py:82
  86.4 2.8 %fusion.41 = bf16[128,512]{1,0:T(8,128)(2,1)S(1)} fusion(bf16[128,2688]{0,1:T(8,128)(2,1)S(1)} %all_gather.11, bf16[1,512,2688]{2,1,0:T(8,128)(2,1)} %param.21), kind=kOutput, calls=%fused_computation.52 | convolution fusion | flops 352387072 | bytes 3571712 | tf_op jit(solution)/shard_map/dot_general | solution.py:52
  92.1 1.6 fusion.77
  93.6 2.2 %fusion.29 = f32[2,2,128,512]{2,3,1,0:T(8,128)} fusion(bf16[512,2,128,1]{0,2,3,1:T(8,128)(2,1)S(1)} %bitcast.142, pred[128,512]{0,1:T(8,128)(4,1)S(1)} %get-tuple-element.18, bf16[128,2,2,128]{3,2,1,0:T(2,128)(2,1)} %reshape.78), kind=kOutput, calls=%fused_computation.40 | convolution fusion | flops 67633152 | bytes 1507328 | tf_op jit(solution)/shard_map/qhgd,khd->hgqk/dot_general | solution.py:26
  95.9 2.0 %convolution_convert_fusion.1 = bf16[2,128,2,128]{3,1,2,0:T(8,128)(2,1)S(1)} fusion(bf16[512,2,128,1]{0,2,3,1:T(8,128)(2,1)} %bitcast.148, f32[2,2,128]{2,1,0:T(2,128)S(1)} %fusion.77, f32[2,2,128,512]{2,3,1,0:T(8,128)} %fusion.29), kind=kOutput, calls=%fused_computation.51 | convolution fusion | flops 67961856 | bytes 1443840 | tf_op jit(solution)/shard_map/hgqk,khd->qhgd/dot_general | solution.py:129
  97.9 3.9 %convolution_convert_fusion = bf16[128,2688]{0,1:T(8,128)(2,1)} fusion(bf16[128,512]{0,1:T(8,128)(2,1)S(1)} %bitcast.149, bf16[1,512,2688]{2,1,0:T(8,128)(2,1)} %param.21), kind=kOutput, calls=%fused_computation.5 | convolution fusion | flops 352665600 | bytes 3571712 | tf_op jit(solution)/shard_map/dot_general | solution.py:133
  101.9 1.5 fusion.80
  103.4 1.8 %fusion.45 = f32[2,128,512,1]{2,1,3,0:T(8,128)S(1)} fusion(bf16[128,2,2,128]{0,3,2,1:T(8,128)(2,1)} %bitcast.150, f32[2,2,128]{2,1,0:T(2,128)S(1)} %get-tuple-element.21, bf16[512,2,128,1]{0,2,3,1:T(8,128)(2,1)} %bitcast.139, bf16[128,2,2,128]{0,3,2,1:T(8,128)(2,1)} %bitcast.144, pred[128,512]{0,1:T(8,128)(4,1)S(1)} %copy-done.13), kind=kOutput, calls=%fused_computation.58 | convolution fusion | flops 135529472 | bytes 1116160 | tf_op jit(solution)/shard_map/hgqk,qhgd->khd/dot_general | solution.py:155
  105.3 1.8 %multiply_reduce_fusion = (f32[2,2,128]{2,1,0:T(2,128)S(1)}, f32[2,2,128,512]{2,3,1,0:T(8,128)S(1)}) fusion(f32[2,2,128,512]{2,3,1,0:T(8,128)} %get-tuple-element.22, f32[2,2,128]{2,1,0:T(2,128)S(1)} %get-tuple-element.21, bf16[512,2,128,1]{0,2,3,1:T(8,128)(2,1)} %bitcast.147, bf16[128,2,2,128]{0,3,2,1:T(8,128)(2,1)} %bitcast.151), kind=kOutput, calls=%fused_computation.56 | convolution fusion | flops 67894784 | bytes 2494464 | tf_op jit(solution)/shard_map/qhgd,khd->hgqk/dot_general | solution.py:158
  108.5 1.3 collective-permute-start.7
  109.8 1.3 collective-permute-start.6
  114.8 2.8 %collective-permute-done.6 = bf16[128,512]{0,1:T(8,128)(2,1)S(1)} collective-permute-done((bf16[128,512]{0,1:T(8,128)(2,1)S(1)}, bf16[128,512]{0,1:T(8,128)(2,1)S(1)}, u32[]{:S(2)}, u32[]{:S(2)}) %collective-permute-start.6) | collective-permute-done | bytes 131104 | tf_op jit(solution)/shard_map/ppermute | solution.py:16
  119.0 1.4 fusion.2
  120.5 5.5 %reduce-scatter.3.cloned.1.call-done = bf16[128,672]{0,1:T(8,128)(2,1)} async-done(((bf16[128,2688]{0,1:T(8,128)(2,1)}), bf16[128,672]{0,1:T(8,128)(2,1)}) %reduce-scatter.3.cloned.1.call-update) | async-done | bytes 172048 | tf_op jit(solution)/shard_map/reduce_scatter | solution.py:134
  126.0 1.6 fusion.56
  127.7 22.2 %reduce-scatter.5.cloned.1.call-done = bf16[128,672]{0,1:T(8,128)(2,1)} async-done(((bf16[128,2688]{0,1:T(8,128)(2,1)}), bf16[128,672]{0,1:T(8,128)(2,1)}) %reduce-scatter.5.cloned.1.call-update) | async-done | bytes 172048 | tf_op jit(solution)/shard_map/reduce_scatter | solution.py:186
  151.0 9.7 %psum.7 = f32[128,1]{0,1:T(1,128)S(1)} all-reduce(f32[128,1]{0,1:T(1,128)S(1)} %bitcast.156), channel_id=1, replica_groups=mesh['pipe'=2,'seq'=4,'fsdp'=4] {'fsdp'}, use_global_device_ids=true, to_apply=%region_10.11 | all-reduce | flops 128 | bytes 1024 | tf_op jit(solution)/shard_map/psum | solution.py:192
  160.6 1.8 %fusion.57 = bf16[1,128,672]{1,2,0:T(8,128)(2,1)} fusion(bf16[128,672]{0,1:T(8,128)(2,1)} %reduce-scatter.5.cloned.1.call-done, bf16[128,672]{0,1:T(8,128)(2,1)S(1)} %broadcast_select_fusion, bf16[1,128,672]{1,2,0:T(8,128)(2,1)S(1)} %copy-done.3, f32[128]{0:T(128)S(1)} %multiply_bitcast_fusion, f32[128]{0:T(128)S(1)} %get-tuple-element.19, ...), kind=kLoop, calls=%fused_computation.80 | loop fusion | flops 860160 | bytes 692352 | tf_op jit(solution)/shard_map/broadcast_in_dim | solution.py:195
  (82 shorter events, 23.9 us)
Async XLA Ops:
  7.2 59.1 %copy-start = (bf16[1,2688,512]{2,1,0:T(8,128)(2,1)S(1)}, bf16[1,2688,512]{2,1,0:T(8,128)(2,1)}, u32[]{:S(2)}) copy-start(bf16[1,2688,512]{2,1,0:T(8,128)(2,1)} %param.18) | copy-start | bytes 8257540
  7.2 26.8 %copy-start.15 = (s32[1,512]{1,0:T(1,128)S(1)}, s32[1,512]{1,0:T(1,128)}, u32[]{:S(2)}) copy-start(s32[1,512]{1,0:T(1,128)} %param.23) | copy-start | bytes 6148
  7.2 26.8 %copy-start.16 = (s32[1,512]{1,0:T(1,128)S(1)}, s32[1,512]{1,0:T(1,128)}, u32[]{:S(2)}) copy-start(s32[1,512]{1,0:T(1,128)} %param.22) | copy-start | bytes 6148
  7.2 27.0 %copy-start.14 = (f32[1,2688]{1,0:T(1,128)S(1)}, f32[1,2688]{1,0:T(1,128)}, u32[]{:S(2)}) copy-start(f32[1,2688]{1,0:T(1,128)} %param.17) | copy-start | bytes 32260
  7.2 118.8 %reduce-scatter.3.cloned.1.call-start = ((), (), s32[]{:S(2)}) async-start(), calls=%async_computation.2 | async-start | bytes 860160 | tf_op jit(solution)/shard_map/reduce_scatter | solution.py:134
  7.3 28.5 %collective-permute-start = (bf16[128,672]{0,1:T(8,128)(2,1)}, bf16[128,672]{0,1:T(8,128)(2,1)}, u32[]{:S(2)}, u32[]{:S(2)}) collective-permute-start(bf16[128,672]{0,1:T(8,128)(2,1)} %bitcast.157), channel_id=1, source_target_pairs={{0,16},{1,17},{2,18},{3,19},{4,20},{5,21},{6,22},{7,23},{8,24},{9,... | collective-permute-start | bytes 516104 | tf_op jit(solution)/shard_map/ppermute | solution.py:16
  13.0 55.7 %collective-permute-start.4 = (bf16[128,672]{0,1:T(8,128)(2,1)}, bf16[128,672]{0,1:T(8,128)(2,1)}, u32[]{:S(2)}, u32[]{:S(2)}) collective-permute-start(bf16[128,672]{0,1:T(8,128)(2,1)} %bitcast.158), channel_id=1, source_target_pairs={{16,0},{17,1},{18,2},{19,3},{20,4},{21,5},{22,6},{23,7},{24,8},{25... | collective-permute-start | bytes 516104 | tf_op jit(solution)/shard_map/ppermute | solution.py:16
  54.1 1.3 copy-start.4
  58.2 31.7 %collective-permute-start.3 = (bf16[128,1024]{0,1:T(8,128)(2,1)}, bf16[128,1024]{0,1:T(8,128)(2,1)}, u32[]{:S(2)}, u32[]{:S(2)}) collective-permute-start(bf16[128,1024]{0,1:T(8,128)(2,1)} %pad_maximum_fusion.5), channel_id=1, source_target_pairs={{0,4},{4,8},{8,12},{1,5},{5,9},{9,13},{2,6},{6,10},{10,14},{3,7},{... | collective-permute-start | bytes 786440 | tf_op jit(solution)/shard_map/ppermute | solution.py:16
  60.2 29.7 %collective-permute-start.2 = (bf16[128,1024]{0,1:T(8,128)(2,1)}, bf16[128,1024]{0,1:T(8,128)(2,1)}, u32[]{:S(2)}, u32[]{:S(2)}) collective-permute-start(bf16[128,1024]{0,1:T(8,128)(2,1)} %pad_maximum_fusion.5), channel_id=1, source_target_pairs={{0,8},{4,12},{1,9},{5,13},{2,10},{6,14},{3,11},{7,15},{16,24},{20,... | collective-permute-start | bytes 786440 | tf_op jit(solution)/shard_map/ppermute | solution.py:16
  64.3 25.7 %collective-permute-start.1 = (bf16[128,1024]{0,1:T(8,128)(2,1)}, bf16[128,1024]{0,1:T(8,128)(2,1)}, u32[]{:S(2)}, u32[]{:S(2)}) collective-permute-start(bf16[128,1024]{0,1:T(8,128)(2,1)} %pad_maximum_fusion.5), channel_id=1, source_target_pairs={{0,12},{1,13},{2,14},{3,15},{16,28},{17,29},{18,30},{19,31}} | collective-permute-start | bytes 786440 | tf_op jit(solution)/shard_map/ppermute | solution.py:16
  92.1 9.8 %copy-start.9 = (bf16[512,256]{0,1:T(8,128)(2,1)}, bf16[512,256]{0,1:T(8,128)(2,1)S(1)}, u32[]{:S(2)}) copy-start(bf16[512,256]{0,1:T(8,128)(2,1)S(1)} %get-tuple-element.3) | copy-start | bytes 786436
  97.9 4.0 %copy-start.11 = (bf16[128,512]{0,1:T(8,128)(2,1)S(1)}, bf16[128,512]{0,1:T(8,128)(2,1)}, u32[]{:S(2)}) copy-start(bf16[128,512]{0,1:T(8,128)(2,1)} %copy.43) | copy-start | bytes 393220
  97.9 4.0 %copy-start.13 = (pred[128,512]{0,1:T(8,128)(4,1)S(1)}, pred[128,512]{0,1:T(8,128)(4,1)}, u32[]{:S(2)}) copy-start(pred[128,512]{0,1:T(8,128)(4,1)} %get-tuple-element.17) | copy-start | bytes 196612
  101.8 48.0 %reduce-scatter.5.cloned.1.call-start = ((), (), s32[]{:S(2)}) async-start(), calls=%async_computation.3 | async-start | bytes 860160 | tf_op jit(solution)/shard_map/reduce_scatter | solution.py:186
  105.2 1.8 %copy-start.8 = (f32[2,2,128,512]{2,3,1,0:T(8,128)S(1)}, f32[2,2,128,512]{2,3,1,0:T(8,128)}, u32[]{:S(2)}) copy-start(f32[2,2,128,512]{2,3,1,0:T(8,128)} %get-tuple-element.22) | copy-start | bytes 3145732
  108.3 4.1 %copy-start.10 = (bf16[512,256]{0,1:T(8,128)(2,1)S(1)}, bf16[512,256]{0,1:T(8,128)(2,1)}, u32[]{:S(2)}) copy-start(bf16[512,256]{0,1:T(8,128)(2,1)} %copy-done.9) | copy-start | bytes 786436
  108.5 6.3 %collective-permute-start.7 = (bf16[128,512]{0,1:T(8,128)(2,1)S(1)}, bf16[128,512]{0,1:T(8,128)(2,1)S(1)}, u32[]{:S(2)}, u32[]{:S(2)}) collective-permute-start(bf16[128,512]{0,1:T(8,128)(2,1)S(1)} %get-tuple-element.7), channel_id=1, source_target_pairs={{12,0},{13,1},{14,2},{15,3},{28,16},{29,17},{30,18},{31,19}} | collective-permute-start | bytes 393224 | tf_op jit(solution)/shard_map/ppermute | solution.py:16
  109.8 7.8 %collective-permute-start.6 = (bf16[128,512]{0,1:T(8,128)(2,1)S(1)}, bf16[128,512]{0,1:T(8,128)(2,1)S(1)}, u32[]{:S(2)}, u32[]{:S(2)}) collective-permute-start(bf16[128,512]{0,1:T(8,128)(2,1)S(1)} %get-tuple-element.8), channel_id=1, source_target_pairs={{8,0},{12,4},{9,1},{13,5},{10,2},{14,6},{11,3},{15,7},{24,16},{28,... | collective-permute-start | bytes 393224 | tf_op jit(solution)/shard_map/ppermute | solution.py:16
  111.1 6.5 %collective-permute-start.5 = (bf16[128,512]{0,1:T(8,128)(2,1)S(1)}, bf16[128,512]{0,1:T(8,128)(2,1)S(1)}, u32[]{:S(2)}, u32[]{:S(2)}) collective-permute-start(bf16[128,512]{0,1:T(8,128)(2,1)S(1)} %get-tuple-element.6), channel_id=1, source_target_pairs={{4,0},{8,4},{12,8},{5,1},{9,5},{13,9},{6,2},{10,6},{14,10},{7,3},{... | collective-permute-start | bytes 393224 | tf_op jit(solution)/shard_map/ppermute | solution.py:16
  113.5 4.1 %copy-start.5 = (bf16[1,2688,256]{2,1,0:T(8,128)(2,1)S(1)}, bf16[1,2688,256]{2,1,0:T(8,128)(2,1)}, u32[]{:S(2)}) copy-start(bf16[1,2688,256]{2,1,0:T(8,128)(2,1)} %param.19) | copy-start | bytes 4128772
  117.6 1.4 copy-start.7
  119.0 7.0 %copy-start.2 = (bf16[128,672]{0,1:T(8,128)(2,1)S(1)}, bf16[128,672]{0,1:T(8,128)(2,1)}, u32[]{:S(2)}) copy-start(bf16[128,672]{0,1:T(8,128)(2,1)} %copy-done.1) | copy-start | bytes 516100
  119.0 30.9 %copy-start.3 = (bf16[1,128,672]{1,2,0:T(8,128)(2,1)S(1)}, bf16[1,128,672]{1,2,0:T(8,128)(2,1)}, u32[]{:S(2)}) copy-start(bf16[1,128,672]{1,2,0:T(8,128)(2,1)} %param.14) | copy-start | bytes 516100
  (3 other events, 2.9 us)
Sparse Core Ops, SparseCore 0:
  102.0 24.0 reduce-scatter.2
  128.4 21.4 reduce-scatter.4
where the time goes:
time: 170 us; the launch traced here: 169 us
  blocking collectives  61.5 us (36%)
  waiting for transfers between devices  31.8 us (19%)
  matrix products  23.2 us (14%)
  starting transfers between devices  19.1 us (11%)
  between operations  14.4 us (8%)
  other arithmetic  11.9 us (7%)
  local copies, waits for them, and re-layouts  7.3 us (4%)
    reduce_scatter x1, waiting for transfers between devices, per_device(): lax.psum_scatter(d_norm.astype(jnp.bfloat16), 'fsdp', scatter_dimension=1...  22.2 us
    ppermute x8, starting transfers between devices, from_behind(): lax.ppermute(value, axis, [(source, source + steps) for source in range(i...  19 us
    all_gather x1, blocking collectives, per_device(): lax.all_gather(stashed[0], 'fsdp', axis=1, tiled=True)  18.8 us
    all_gather x1, blocking collectives, per_device(): lax.all_gather(upstream, 'fsdp', axis=1, tiled=True)  16.7 us
    all_gather x1, blocking collectives, per_device(): lax.all_gather(incoming, 'fsdp', axis=1, tiled=True)  16.3 us
    psum x1, blocking collectives, per_device(): row_mean = lax.psum(row_part, 'fsdp') / MODEL_WIDTH  9.66 us
    dot_general x4, matrix products, contract_last(): lax.dot_general(left, right, (((1,), (1,)), ((), ())), preferred_element_...  5.57 us
    reduce_scatter x1, waiting for transfers between devices, per_device(): lax.psum_scatter(partial_out.astype(jnp.bfloat16), 'fsdp', scatter_dimens...  5.53 us
  transfers between devices with their start and end apart: 10, of which 4 were waited for; matrix products, arithmetic and copies ran while one was open for 14% of the time, Pallas kernels for 0%

commit v1 on v0

v1 whole, which is shorter than its diff:
```python
import functools

import jax
import jax.numpy as jnp
from jax import lax
from jax.experimental import pallas as pl
from jax.experimental.pallas import tpu as pltpu
from jax.sharding import PartitionSpec as P

MODEL_WIDTH = 2688
HEAD_SIZE = 128
WINDOW_TOKENS = 512
MESH = pl.DeviceIdType.MESH
F32 = jnp.float32
BF16 = jnp.bfloat16
STASH, UP, ROWS = 0, 1, 2
BWD, FWD = 0, 1


def nn(left, right):
    return lax.dot_general(left, right, (((1,), (0,)), ((), ())), preferred_element_type=F32)


def nt(left, right):
    return lax.dot_general(left, right, (((1,), (1,)), ((), ())), preferred_element_type=F32)


def tn(left, right):
    return lax.dot_general(left, right, (((0,), (0,)), ((), ())), preferred_element_type=F32)


def kernel(
    sizes,
    embedded,
    sent_forward,
    stashed,
    sent_backward,
    loss_grad,
    gain_ref,
    w_query,
    w_key,
    w_value,
    w_out,
    docs_fwd,
    docs_bwd,
    forward_out,
    input_grad,
    wq,
    wk,
    wv,
    wo,
    gathered,
    gain_parts,
    kv_window,
    q_rows,
    probs,
    terms,
    pair_out,
    pair_in,
    chip_out,
    chip_in,
    part,
    rs_out,
    rs_in,
    stat_out,
    stat_in,
    local_sem,
    send_sem,
    gather_sem,
    pipe_sem,
    kv_sem,
    pair_sem,
    chip_sem,
    rs_sem,
    stat_sem,
):
    sections, chips, groups, reach = sizes
    length, share = embedded.shape
    section = lax.axis_index("pipe")
    seq = lax.axis_index("seq")
    z = lax.axis_index("fsdp")
    chip, core = seq // 2, lax.rem(seq, 2)
    sibling = seq + 1 - 2 * core
    slots = 2 * (reach + 1)
    scale = HEAD_SIZE ** (-0.5)
    pending = []

    def when(cond, action):
        pl.when(cond)(action)

    def remote(src, dst, recv, target):
        index = len(pending)
        copy = pltpu.make_async_remote_copy(
            src_ref=src,
            dst_ref=dst,
            send_sem=send_sem.at[index],
            recv_sem=recv,
            device_id=target,
            device_id_type=MESH,
        )
        return copy

    def send(cond, src, dst, recv, target):
        copy = remote(src, dst, recv, target)
        pending.append((cond, copy))
        when(cond, lambda: copy.start())

    def arrive(cond, dst, recv, target):
        copy = pltpu.make_async_remote_copy(
            src_ref=dst,
            dst_ref=dst,
            send_sem=send_sem.at[0],
            recv_sem=recv,
            device_id=target,
            device_id_type=MESH,
        )
        when(cond, lambda: copy.wait_recv())

    def local(src, dst, index):
        return pltpu.make_async_copy(src, dst, local_sem.at[index])

    own_stash = local(stashed.at[0], gathered.at[STASH, z], 0)
    own_up = local(loss_grad, gathered.at[UP, z], 1)
    own_rows = local(embedded, gathered.at[ROWS, z], 2)
    weights = [
        local(w_key.at[0], wk, 3),
        local(w_value.at[0], wv, 4),
        local(w_query.at[0], wq, 5),
        local(w_out.at[0], wo, 6),
    ]
    own_stash.start()
    when(section == sections - 1, lambda: own_up.start())
    when(section == 0, lambda: own_rows.start())
    for copy in weights:
        copy.start()

    barrier = pltpu.get_barrier_semaphore()
    neighbours = [
        (z > 0, {"fsdp": z - 1}),
        (z < groups - 1, {"fsdp": z + 1}),
        (section > 0, {"pipe": section - 1}),
        (section < sections - 1, {"pipe": section + 1}),
        (seq >= 0, {"seq": sibling}),
    ]
    for e in range(1, reach + 1):
        neighbours.append((chip >= e, {"seq": seq - 2 * e}))
        neighbours.append((chip + e < chips, {"seq": seq + 2 * e}))
    for d in range(2, groups):
        neighbours.append((z - d >= 0, {"fsdp": z - d}))
        neighbours.append((z + d < groups, {"fsdp": z + d}))
    total = jnp.int32(0)
    for cond, target in neighbours:
        total = total + cond.astype(jnp.int32)

        def greet(target=target):
            pl.semaphore_signal(barrier, inc=1, device_id=target, device_id_type=MESH)

        when(cond, greet)
    pl.semaphore_wait(barrier, total)

    send(
        section > 0,
        sent_backward.at[0],
        gathered.at[UP, z],
        pipe_sem.at[0],
        {"pipe": section - 1},
    )
    send(
        section < sections - 1,
        sent_forward.at[0],
        gathered.at[ROWS, z],
        pipe_sem.at[1],
        {"pipe": section + 1},
    )

    def gather_from(array, distance):
        low, high = z - distance, z + distance
        if distance:
            arrive(low >= 0, gathered.at[array, low], gather_sem.at[array, low], {"fsdp": z - 1})
        send(
            (low >= 0) & (z < groups - 1),
            gathered.at[array, low],
            gathered.at[array, low],
            gather_sem.at[array, low],
            {"fsdp": z + 1},
        )
        if distance:
            arrive(
                high < groups, gathered.at[array, high], gather_sem.at[array, high], {"fsdp": z + 1}
            )
        send(
            (high < groups) & (z > 0),
            gathered.at[array, high],
            gathered.at[array, high],
            gather_sem.at[array, high],
            {"fsdp": z - 1},
        )

    def whole_rows(array):
        return jnp.concatenate([gathered[array, j] for j in range(groups)], axis=1)

    gain = gain_ref[...]

    def project(array, which):
        rows = whole_rows(array).astype(F32)
        row_scale = lax.rsqrt(jnp.mean(rows * rows, axis=-1, keepdims=True) + 1e-06)
        h = (rows * row_scale * gain).astype(BF16)
        half = wk.shape[1]
        kv_window[which, core, :, :half] = nn(h, wk[...]).astype(BF16)
        kv_window[which, core, :, half:] = nn(h, wv[...]).astype(BF16)
        spread(which)
        q_rows[which] = nn(h, wq[...]).astype(BF16)
        return row_scale

    def spread(which):
        for e in range(1, reach + 1):
            slot = 2 * e + core
            send(
                chip + e < chips,
                kv_window.at[which, core],
                kv_window.at[which, slot],
                kv_sem.at[which, slot],
                {"seq": seq + 2 * e},
            )
        send(
            core == 0,
            kv_window.at[which, core],
            kv_window.at[which, core],
            kv_sem.at[which, core],
            {"seq": sibling},
        )

    def share_pair(which):
        for e in range(1, reach + 1):
            slot = 2 * e + core
            arrive(
                chip >= e, kv_window.at[which, slot], kv_sem.at[which, slot], {"seq": sibling}
            )
            send(
                chip >= e,
                kv_window.at[which, slot],
                kv_window.at[which, slot],
                kv_sem.at[which, slot],
                {"seq": sibling},
            )

    def take_pair(which):
        arrive(core == 1, kv_window.at[which, 0], kv_sem.at[which, 0], {"seq": sibling})
        for e in range(1, reach + 1):
            slot = 2 * e + 1 - core
            arrive(
                chip >= e, kv_window.at[which, slot], kv_sem.at[which, slot], {"seq": sibling}
            )

    def clear_absent():
        for which in (BWD, FWD):

            def clear(slot, which=which):
                kv_window[which, slot] = jnp.zeros(kv_window.shape[2:], BF16)

            when(core == 0, lambda: clear(1))
            for e in range(1, reach + 1):

                def both(e=e):
                    clear(2 * e)
                    clear(2 * e + 1)

                when(chip < e, both)

    def keep_mask(docs):
        start = pl.multiple_of(seq * length, 128)
        own = docs[:, pl.ds(start, length)].astype(F32)
        own_docs = jnp.transpose(jnp.broadcast_to(own, (length, length)))
        q_pos = seq * length + lax.broadcasted_iota(jnp.int32, (length, length), 0)
        pieces = []
        for slot in range(slots):
            first = (2 * (chip - slot // 2) + slot % 2) * length
            at = pl.multiple_of(jnp.maximum(first, 0), 128)
            other = docs[:, pl.ds(at, length)].astype(F32)
            k_pos = first + lax.broadcasted_iota(jnp.int32, (length, length), 1)
            keep = (k_pos >= 0) & (k_pos <= q_pos) & (q_pos - k_pos < WINDOW_TOKENS)
            keep = keep & (own_docs == jnp.broadcast_to(other, (length, length)))
            pieces.append(jnp.where(keep, 0.0, -1e30))
        bias = jnp.concatenate(pieces, axis=1)
        return jnp.concatenate([bias, bias], axis=0)

    def window_part(which, column):
        return jnp.concatenate(
            [
                kv_window[which, slot, :, column * HEAD_SIZE : (column + 1) * HEAD_SIZE]
                for slot in range(slots)
            ],
            axis=0,
        )

    def pair_rows(values, head):
        low = 2 * head * HEAD_SIZE
        return jnp.concatenate(
            [values[:, low : low + HEAD_SIZE], values[:, low + HEAD_SIZE : low + 2 * HEAD_SIZE]],
            axis=0,
        )

    kv_heads = wk.shape[1] // HEAD_SIZE

    def softmax(which, head, bias):
        queries = pair_rows(q_rows[which], head)
        scores = nt(queries, window_part(which, head)) * scale
        scores = jnp.where(bias < 0.0, bias, scores)
        top = jnp.max(scores, axis=-1, keepdims=True)
        expo = jnp.exp(scores - top)
        return expo / jnp.sum(expo, axis=-1, keepdims=True)

    def scatter_from(which, distance):
        high, low = z + distance, z - distance
        for side, at, cond, more, target in (
            (0, high, high < groups, z > 0, {"fsdp": z + 1}),
            (1, low, low >= 0, z < groups - 1, {"fsdp": z - 1}),
        ):

            arrive(cond & more, rs_in.at[which, side, at], rs_sem.at[which, side, at], target)

            def added(side=side, at=at):
                rs_out[which, side, at] = (
                    part[which, at] + rs_in[which, side, at].astype(F32)
                ).astype(BF16)

            def alone(side=side, at=at):
                rs_out[which, side, at] = part[which, at].astype(BF16)

            when(cond & more, added)
            when(cond & jnp.logical_not(more), alone)
            send(
                cond,
                rs_out.at[which, side, at],
                rs_in.at[which, side, at],
                rs_sem.at[which, side, at],
                target,
            )

    def scatter_total(which):
        for side, more, source in (
            (0, z > 0, {"fsdp": z - 1}),
            (1, z < groups - 1, {"fsdp": z + 1}),
        ):
            arrive(more, rs_in.at[which, side, z], rs_sem.at[which, side, z], source)

            def add(side=side):
                part[which, z] = part[which, z] + rs_in[which, side, z].astype(F32)

            when(more, add)
        return part[which, z]

    def split_part(which, values):
        for j in range(groups):
            part[which, j] = values[:, j * share : (j + 1) * share]

    own_stash.wait()
    gather_from(STASH, 0)
    when(section == sections - 1, lambda: own_up.wait())
    arrive(section < sections - 1, gathered.at[UP, z], pipe_sem.at[0], {"pipe": section})
    gather_from(UP, 0)
    clear_absent()
    for j in range(groups):
        gain_parts[j] = gain[:, j * share : (j + 1) * share]
    for d in range(1, groups):
        gather_from(STASH, d)
    gather_from(UP, 1)
    when(section == 0, lambda: own_rows.wait())
    arrive(section > 0, gathered.at[ROWS, z], pipe_sem.at[1], {"pipe": section})
    gather_from(ROWS, 0)
    for copy in weights[:3]:
        copy.wait()

    scale_backward = project(STASH, BWD)
    gather_from(UP, 2) if groups > 2 else None
    share_pair(BWD)
    bias = keep_mask(docs_bwd)
    take_pair(BWD)
    for head in range(kv_heads):
        probs[head] = softmax(BWD, head, bias)
    for d in range(3, groups):
        gather_from(UP, d)
    gather_from(ROWS, 1)
    weights[3].wait()
    d_attn = nt(whole_rows(UP), wo[...]).astype(BF16)
    dq_parts = []
    for head in range(kv_heads):
        p = probs[head]
        gradient = pair_rows(d_attn, head)
        keys = window_part(BWD, head)
        dp = nt(gradient, window_part(BWD, kv_heads + head))
        delta = jnp.sum(p * dp, axis=-1, keepdims=True)
        ds = (p * (dp - delta)).astype(BF16)
        dk = tn(ds, pair_rows(q_rows[BWD], head)) * scale
        dv = tn(p.astype(BF16), gradient)
        for slot in range(slots):
            low = head * HEAD_SIZE
            rows = slice(slot * length, (slot + 1) * length)
            terms[slot, :, low : low + HEAD_SIZE] = dk[rows]
            low = low + kv_heads * HEAD_SIZE
            terms[slot, :, low : low + HEAD_SIZE] = dv[rows]
        dq = (nn(ds, keys) * scale).astype(BF16)
        dq_parts += [dq[:length], dq[length:]]
    for e in list(range(1, reach + 1)) + [0]:
        cond = (chip >= e) if e else (core == 1)

        def stage(e=e):
            pair_out[e] = terms[2 * e + 1 - core].astype(BF16)

        when(cond, stage)
        send(cond, pair_out.at[e], pair_in.at[e], pair_sem.at[e], {"seq": sibling})
    for e in range(1, reach + 1):
        arrive(chip >= e, pair_in.at[e], pair_sem.at[e], {"seq": sibling})

        def stage(e=e):
            chip_out[e - 1] = (terms[2 * e + core] + pair_in[e].astype(F32)).astype(BF16)

        when(chip >= e, stage)
        send(
            chip >= e,
            chip_out.at[e - 1],
            chip_in.at[e - 1],
            chip_sem.at[e - 1],
            {"seq": seq - 2 * e},
        )
    gather_from(ROWS, 2) if groups > 2 else None
    dq_local = jnp.concatenate(dq_parts, axis=1)
    d_norm = nt(dq_local, wq[...])
    arrive(core == 0, pair_in.at[0], pair_sem.at[0], {"seq": sibling})

    def add_pair():
        terms[core] = terms[core] + pair_in[0].astype(F32)

    when(core == 0, add_pair)
    for e in range(1, reach + 1):
        arrive(chip + e < chips, chip_in.at[e - 1], chip_sem.at[e - 1], {"seq": sibling})

        def add_chip(e=e):
            terms[core] = terms[core] + chip_in[e - 1].astype(F32)

        when(chip + e < chips, add_chip)
    owned = terms[core].astype(BF16)
    half = wk.shape[1]
    d_norm = d_norm + nt(owned[:, :half], wk[...]) + nt(owned[:, half:], wv[...])
    split_part(BWD, d_norm)
    for d in range(groups - 1, 0, -1):
        if d == 1:
            for far in range(3, groups):
                gather_from(ROWS, far)
        scatter_from(BWD, d)
    rows = whole_rows(STASH).astype(F32)
    row_part = jnp.sum(rows * gain * d_norm, axis=-1, keepdims=True)
    stat_out[...] = jnp.transpose(jnp.broadcast_to(row_part, (length, length)))[:8]
    for d in range(1, groups):
        for cond, other in ((z + d < groups, z + d), (z - d >= 0, z - d)):
            send(cond, stat_out, stat_in.at[z], stat_sem.at[z], {"fsdp": other})

    project(ROWS, FWD)
    share_pair(FWD)
    bias = keep_mask(docs_fwd)
    take_pair(FWD)
    attn_parts = []
    for head in range(kv_heads):
        p = softmax(FWD, head, bias).astype(BF16)
        attn = nn(p, window_part(FWD, kv_heads + head)).astype(BF16)
        attn_parts += [attn[:length], attn[length:]]
    split_part(FWD, nn(jnp.concatenate(attn_parts, axis=1), wo[...]))
    for d in range(groups - 1, 0, -1):
        scatter_from(FWD, d)

    d_share = scatter_total(BWD)
    stat_in[z] = stat_out[...]
    for d in range(1, groups):
        for cond, other in ((z + d < groups, z + d), (z - d >= 0, z - d)):
            arrive(cond, stat_in.at[other], stat_sem.at[other], {"fsdp": other})
    stat = stat_in[0]
    for j in range(1, groups):
        stat = stat + stat_in[j]
    stat = jnp.broadcast_to(stat[:1], (length, length))
    row_mean = jnp.transpose(stat)[:, :1] / MODEL_WIDTH
    own = gathered[STASH, z].astype(F32)
    d_input = scale_backward * gain_parts[z] * d_share - own * scale_backward**3 * row_mean
    input_grad[0] = (gathered[UP, z].astype(F32) + d_input).astype(BF16)
    summed = scatter_total(FWD)
    forward_out[0] = (gathered[ROWS, z].astype(F32) + summed).astype(BF16)
    for cond, copy in pending:
        when(cond, lambda copy=copy: copy.wait_send())


def per_device(*args):
    embedded = args[0]
    length, share = embedded.shape
    w_query, w_key, w_out = args[6], args[7], args[9]
    sections = lax.axis_size("pipe")
    chips = lax.axis_size("seq") // 2
    groups = lax.axis_size("fsdp")
    hops = min(WINDOW_TOKENS // length, lax.axis_size("seq") - 1)
    reach = min((hops + 1) // 2, chips - 1)
    slots = 2 * (reach + 1)
    width = w_key.shape[2]
    kv_heads = width // HEAD_SIZE
    anywhere = pl.BlockSpec(memory_space=pl.ANY)
    inside = pl.BlockSpec(memory_space=pltpu.VMEM)
    sent = jax.ShapeDtypeStruct((1, length, share), BF16)
    dma = pltpu.SemaphoreType.DMA
    call = pl.pallas_call(
        functools.partial(kernel, (sections, chips, groups, reach)),
        out_shape=(sent, sent),
        in_specs=[anywhere] * 5 + [inside] + [anywhere] * 4 + [inside] * 2,
        out_specs=(inside, inside),
        scratch_shapes=[
            pltpu.VMEM(w_query.shape[1:], BF16),
            pltpu.VMEM(w_key.shape[1:], BF16),
            pltpu.VMEM(w_key.shape[1:], BF16),
            pltpu.VMEM(w_out.shape[1:], BF16),
            pltpu.VMEM((3, groups, length, share), BF16),
            pltpu.VMEM((groups, 1, share), F32),
            pltpu.VMEM((2, slots, length, 2 * width), BF16),
            pltpu.VMEM((2, length, w_query.shape[2]), BF16),
            pltpu.VMEM((kv_heads, 2 * length, slots * length), F32),
            pltpu.VMEM((slots, length, 2 * width), F32),
            pltpu.VMEM((reach + 1, length, 2 * width), BF16),
            pltpu.VMEM((reach + 1, length, 2 * width), BF16),
            pltpu.VMEM((max(reach, 1), length, 2 * width), BF16),
            pltpu.VMEM((max(reach, 1), length, 2 * width), BF16),
            pltpu.VMEM((2, groups, length, share), F32),
            pltpu.VMEM((2, 2, groups, length, share), BF16),
            pltpu.VMEM((2, 2, groups, length, share), BF16),
            pltpu.VMEM((8, length), F32),
            pltpu.VMEM((groups, 8, length), F32),
            dma((7,)),
            dma((20 * groups + 12 * (reach + 1),)),
            dma((3, groups)),
            dma((2,)),
            dma((2, slots)),
            dma((reach + 1,)),
            dma((max(reach, 1),)),
            dma((2, 2, groups)),
            dma((groups,)),
        ],
        compiler_params=pltpu.CompilerParams(
            collective_id=0, has_side_effects=True, vmem_limit_bytes=56 * 1024 * 1024
        ),
        cost_estimate=pl.CostEstimate(
            flops=4_000_000_000, bytes_accessed=10_000_000, transcendentals=500_000
        ),
    )
    return call(*args)


def solution(mesh):
    placed = (
        P("seq", "fsdp"),
        P("pipe", "seq", "fsdp"),
        P("pipe", "seq", "fsdp"),
        P("pipe", "seq", "fsdp"),
        P("seq", "fsdp"),
        P("pipe", None),
        P("pipe", None, "fsdp"),
        P("pipe", None, "fsdp"),
        P("pipe", None, "fsdp"),
        P("pipe", "fsdp", None),
        P("pipe", None),
        P("pipe", None),
    )
    return jax.shard_map(
        per_device,
        mesh=mesh,
        in_specs=placed,
        out_specs=(P("pipe", "seq", "fsdp"), P("pipe", "seq", "fsdp")),
        check_vma=False,
    )
```

time: 170 us -> 95.8 us (0.56)
  the two profiles are of different devices: /device:TPU:0 before, /device:TPU:13 now
where the time goes in v1:
time: 95.8 us; the launch traced here: 95.2 us
  Pallas kernels  82.4 us (86%)
  local copies, waits for them, and re-layouts  12.1 us (13%)
    pallas_call x1, Pallas kernels, per_device(): return call(*args)  82.4 us
    unnamed x5, local copies, waits for them, and re-layouts  8.65 us
    pallas_call x2, local copies, waits for them, and re-layouts, per_device(): return call(*args)  3.46 us

profile of v1, /device:TPU:13, one launch (start us, length us, event | category | flops | bytes accessed | tf_op | source)
XLA Modules:
  0.0 95.2 jit_solution(15460097765947613036)
XLA Ops:
  0.6 1.7 %copy.14.embedded = bf16[128,672]{1,0:T(8,128)(2,1)} copy(bf16[128,672]{0,1:T(8,128)(2,1)} %param.12) | data formatting | bytes 344064 | tf_op args[0]
  2.4 1.7 %copy.15.sent_forward = bf16[1,128,672]{2,1,0:T(8,128)(2,1)} copy(bf16[1,128,672]{1,2,0:T(8,128)(2,1)} %param.13) | data formatting | bytes 344064 | tf_op args[1]
  4.1 1.7 %copy.16.stashed = bf16[1,128,672]{2,1,0:T(8,128)(2,1)} copy(bf16[1,128,672]{1,2,0:T(8,128)(2,1)} %param.14) | data formatting | bytes 344064 | tf_op args[2]
  5.8 1.7 %copy.17.sent_backward = bf16[1,128,672]{2,1,0:T(8,128)(2,1)} copy(bf16[1,128,672]{1,2,0:T(8,128)(2,1)} %param.15) | data formatting | bytes 344064 | tf_op args[3]
  7.6 1.7 %copy.18.loss_grad = bf16[128,672]{1,0:T(8,128)(2,1)} copy(bf16[128,672]{0,1:T(8,128)(2,1)} %param.16) | data formatting | bytes 344064 | tf_op args[4]
  9.3 82.4 %shard_map.131 = (bf16[1,128,672]{2,1,0:T(8,128)(2,1)}, bf16[1,128,672]{2,1,0:T(8,128)(2,1)}) custom-call(bf16[128,672]{1,0:T(8,128)(2,1)} %copy.14.embedded, bf16[1,128,672]{2,1,0:T(8,128)(2,1)} %copy.15.sent_forward, bf16[1,128,672]{2,1,0:T(8,128)(2,1)} %copy.16.stashed, bf16[1,128,672]{2,1,0:T(8,128)(2,1)} %copy.17.sent_backward, ...), custom_call_target="tpu_custom_call" | custom-call | flops 4000000000 | bytes 10000000 | tf_op jit(solution)/shard_map/pallas_call | solution.py:548
  91.7 1.7 %copy.19 = bf16[1,128,672]{1,2,0:T(8,128)(2,1)} copy(bf16[1,128,672]{2,1,0:T(8,128)(2,1)} %get-tuple-element.2) | data formatting | bytes 344064 | tf_op jit(solution)/shard_map/pallas_call | solution.py:548
  93.5 1.7 %copy.20 = bf16[1,128,672]{1,2,0:T(8,128)(2,1)} copy(bf16[1,128,672]{2,1,0:T(8,128)(2,1)} %get-tuple-element.3) | data formatting | bytes 344064 | tf_op jit(solution)/shard_map/pallas_call | solution.py:548

commit v2 on v1

--- a/solution.py
+++ b/solution.py
@@ -50,7 +50,7 @@
     wv,
     wo,
     gathered,
-    gain_parts,
+    gain_columns,
     kv_window,
     q_rows,
     probs,
@@ -75,7 +75,7 @@
     stat_sem,
 ):
     sections, chips, groups, reach = sizes
-    length, share = embedded.shape
+    share, length = embedded.shape
     section = lax.axis_index("pipe")
     seq = lax.axis_index("seq")
     z = lax.axis_index("fsdp")
@@ -173,13 +173,13 @@
         {"pipe": section + 1},
     )
 
-    def gather_from(array, distance):
+    def gather_from(array, distance, source=None):
         low, high = z - distance, z + distance
         if distance:
             arrive(low >= 0, gathered.at[array, low], gather_sem.at[array, low], {"fsdp": z - 1})
         send(
             (low >= 0) & (z < groups - 1),
-            gathered.at[array, low],
+            gathered.at[array, low] if source is None else source,
             gathered.at[array, low],
             gather_sem.at[array, low],
             {"fsdp": z + 1},
@@ -190,21 +190,20 @@
             )
         send(
             (high < groups) & (z > 0),
-            gathered.at[array, high],
+            gathered.at[array, high] if source is None else source,
             gathered.at[array, high],
             gather_sem.at[array, high],
             {"fsdp": z - 1},
         )
 
     def whole_rows(array):
-        return jnp.concatenate([gathered[array, j] for j in range(groups)], axis=1)
-
-    gain = gain_ref[...]
+        return gathered[array].reshape(groups * share, length)
+
 
     def project(array, which):
         rows = whole_rows(array).astype(F32)
-        row_scale = lax.rsqrt(jnp.mean(rows * rows, axis=-1, keepdims=True) + 1e-06)
-        h = (rows * row_scale * gain).astype(BF16)
+        row_scale = lax.rsqrt(jnp.mean(rows * rows, axis=0, keepdims=True) + 1e-06)
+        h = jnp.transpose((rows * row_scale * gain_columns[...]).astype(BF16))
         half = wk.shape[1]
         kv_window[which, core, :, :half] = nn(h, wk[...]).astype(BF16)
         kv_window[which, core, :, half:] = nn(h, wv[...]).astype(BF16)
@@ -351,17 +350,17 @@
         return part[which, z]
 
     def split_part(which, values):
-        for j in range(groups):
-            part[which, j] = values[:, j * share : (j + 1) * share]
-
-    own_stash.wait()
-    gather_from(STASH, 0)
+        part[which] = values.reshape(groups, share, length)
+
+    gather_from(STASH, 0, stashed.at[0])
     when(section == sections - 1, lambda: own_up.wait())
     arrive(section < sections - 1, gathered.at[UP, z], pipe_sem.at[0], {"pipe": section})
     gather_from(UP, 0)
     clear_absent()
-    for j in range(groups):
-        gain_parts[j] = gain[:, j * share : (j + 1) * share]
+    for low in range(0, groups * share, length):
+        row = jnp.broadcast_to(gain_ref[:, low : low + length], (length, length))
+        gain_columns[low : low + length] = jnp.transpose(row)
+    own_stash.wait()
     for d in range(1, groups):
         gather_from(STASH, d)
     gather_from(UP, 1)
@@ -382,7 +381,7 @@
         gather_from(UP, d)
     gather_from(ROWS, 1)
     weights[3].wait()
-    d_attn = nt(whole_rows(UP), wo[...]).astype(BF16)
+    d_attn = jnp.transpose(nn(wo[...], whole_rows(UP)).astype(BF16))
     dq_parts = []
     for head in range(kv_heads):
         p = probs[head]
@@ -425,7 +424,7 @@
         )
     gather_from(ROWS, 2) if groups > 2 else None
     dq_local = jnp.concatenate(dq_parts, axis=1)
-    d_norm = nt(dq_local, wq[...])
+    d_norm = nt(wq[...], dq_local)
     arrive(core == 0, pair_in.at[0], pair_sem.at[0], {"seq": sibling})
 
     def add_pair():
@@ -441,7 +440,7 @@
         when(chip + e < chips, add_chip)
     owned = terms[core].astype(BF16)
     half = wk.shape[1]
-    d_norm = d_norm + nt(owned[:, :half], wk[...]) + nt(owned[:, half:], wv[...])
+    d_norm = d_norm + nt(wk[...], owned[:, :half]) + nt(wv[...], owned[:, half:])
     split_part(BWD, d_norm)
     for d in range(groups - 1, 0, -1):
         if d == 1:
@@ -449,8 +448,8 @@
                 gather_from(ROWS, far)
         scatter_from(BWD, d)
     rows = whole_rows(STASH).astype(F32)
-    row_part = jnp.sum(rows * gain * d_norm, axis=-1, keepdims=True)
-    stat_out[...] = jnp.transpose(jnp.broadcast_to(row_part, (length, length)))[:8]
+    row_part = jnp.sum(rows * gain_columns[...] * d_norm, axis=0, keepdims=True)
+    stat_out[...] = jnp.broadcast_to(row_part, (8, length))
     for d in range(1, groups):
         for cond, other in ((z + d < groups, z + d), (z - d >= 0, z - d)):
             send(cond, stat_out, stat_in.at[z], stat_sem.at[z], {"fsdp": other})
@@ -464,7 +463,7 @@
         p = softmax(FWD, head, bias).astype(BF16)
         attn = nn(p, window_part(FWD, kv_heads + head)).astype(BF16)
         attn_parts += [attn[:length], attn[length:]]
-    split_part(FWD, nn(jnp.concatenate(attn_parts, axis=1), wo[...]))
+    split_part(FWD, jnp.transpose(nn(jnp.concatenate(attn_parts, axis=1), wo[...])))
     for d in range(groups - 1, 0, -1):
         scatter_from(FWD, d)
 
@@ -476,10 +475,10 @@
     stat = stat_in[0]
     for j in range(1, groups):
         stat = stat + stat_in[j]
-    stat = jnp.broadcast_to(stat[:1], (length, length))
-    row_mean = jnp.transpose(stat)[:, :1] / MODEL_WIDTH
+    row_mean = stat[:1] / MODEL_WIDTH
     own = gathered[STASH, z].astype(F32)
-    d_input = scale_backward * gain_parts[z] * d_share - own * scale_backward**3 * row_mean
+    own_gain = gain_columns[pl.ds(pl.multiple_of(z * share, 16), share)]
+    d_input = scale_backward * own_gain * d_share - own * scale_backward**3 * row_mean
     input_grad[0] = (gathered[UP, z].astype(F32) + d_input).astype(BF16)
     summed = scatter_total(FWD)
     forward_out[0] = (gathered[ROWS, z].astype(F32) + summed).astype(BF16)
@@ -488,8 +487,9 @@
 
 
 def per_device(*args):
+    args = tuple(jnp.swapaxes(arg, -1, -2) for arg in args[:5]) + args[5:]
     embedded = args[0]
-    length, share = embedded.shape
+    share, length = embedded.shape
     w_query, w_key, w_out = args[6], args[7], args[9]
     sections = lax.axis_size("pipe")
     chips = lax.axis_size("seq") // 2
@@ -501,7 +501,7 @@
     kv_heads = width // HEAD_SIZE
     anywhere = pl.BlockSpec(memory_space=pl.ANY)
     inside = pl.BlockSpec(memory_space=pltpu.VMEM)
-    sent = jax.ShapeDtypeStruct((1, length, share), BF16)
+    sent = jax.ShapeDtypeStruct((1, share, length), BF16)
     dma = pltpu.SemaphoreType.DMA
     call = pl.pallas_call(
         functools.partial(kernel, (sections, chips, groups, reach)),
@@ -513,8 +513,8 @@
             pltpu.VMEM(w_key.shape[1:], BF16),
             pltpu.VMEM(w_key.shape[1:], BF16),
             pltpu.VMEM(w_out.shape[1:], BF16),
-            pltpu.VMEM((3, groups, length, share), BF16),
-            pltpu.VMEM((groups, 1, share), F32),
+            pltpu.VMEM((3, groups, share, length), BF16),
+            pltpu.VMEM((groups * share, length), F32),
             pltpu.VMEM((2, slots, length, 2 * width), BF16),
             pltpu.VMEM((2, length, w_query.shape[2]), BF16),
             pltpu.VMEM((kv_heads, 2 * length, slots * length), F32),
@@ -523,9 +523,9 @@
             pltpu.VMEM((reach + 1, length, 2 * width), BF16),
             pltpu.VMEM((max(reach, 1), length, 2 * width), BF16),
             pltpu.VMEM((max(reach, 1), length, 2 * width), BF16),
-            pltpu.VMEM((2, groups, length, share), F32),
-            pltpu.VMEM((2, 2, groups, length, share), BF16),
-            pltpu.VMEM((2, 2, groups, length, share), BF16),
+            pltpu.VMEM((2, groups, share, length), F32),
+            pltpu.VMEM((2, 2, groups, share, length), BF16),
+            pltpu.VMEM((2, 2, groups, share, length), BF16),
             pltpu.VMEM((8, length), F32),
             pltpu.VMEM((groups, 8, length), F32),
             dma((7,)),
@@ -545,7 +545,7 @@
             flops=4_000_000_000, bytes_accessed=10_000_000, transcendentals=500_000
         ),
     )
-    return call(*args)
+    return tuple(jnp.swapaxes(out, 1, 2) for out in call(*args))
 
 
 def solution(mesh):

time: 95.8 us -> 82.9 us (0.87)
  local copies, waits for them, and re-layouts: 12.1 us -> 3.2 us
  Pallas kernels: 82.4 us -> 78.8 us
    unnamed x5 -> x2, local copies, waits for them, and re-layouts: 8.65 us -> 3.2 us
    pallas_call x1, Pallas kernels: 82.4 us -> 78.8 us  [per_device(): return tuple((jnp.swapaxes(out, 1, 2) for out in call(*args)))]
    pallas_call x2 -> x0, local copies, waits for them, and re-layouts: 3.46 us -> none  [per_device(): return call(*args)]
where the time goes in v2:
time: 82.9 us; the launch traced here: 82.7 us
  Pallas kernels  78.8 us (95%)
  local copies, waits for them, and re-layouts  3.2 us (4%)
    pallas_call x1, Pallas kernels, per_device(): return tuple((jnp.swapaxes(out, 1, 2) for out in call(*args)))  78.8 us
    unnamed x2, local copies, waits for them, and re-layouts  3.2 us

profile of v2, /device:TPU:13, one launch (start us, length us, event | category | flops | bytes accessed | tf_op | source)
XLA Modules:
  0.0 82.7 jit_solution(6744804365541841143)
XLA Ops:
  0.6 78.8 %shard_map.131 = (bf16[1,672,128]{2,1,0:T(8,128)(2,1)}, bf16[1,672,128]{2,1,0:T(8,128)(2,1)}) custom-call(bf16[672,128]{1,0:T(8,128)(2,1)} %bitcast.9, bf16[1,672,128]{2,1,0:T(8,128)(2,1)} %bitcast.10, bf16[1,672,128]{2,1,0:T(8,128)(2,1)} %bitcast.11, bf16[1,672,128]{2,1,0:T(8,128)(2,1)} %bitcast.12, bf16[672,128]{1,0:T(8,128)(2,1)} %bitcast.13, ...), custom_call_target="tpu_custom_call" | custom-call | flops 4000000000 | bytes 10000000 | tf_op jit(solution)/shard_map/pallas_call | solution.py:548
  79.5 1.6 %copy.16 = bf16[1,128,672]{1,2,0:T(8,128)(2,1)} copy(bf16[1,128,672]{1,2,0:T(8,128)(2,1)} %bitcast.8) | data formatting | bytes 344064
  81.1 1.6 %copy.17 = bf16[1,128,672]{1,2,0:T(8,128)(2,1)} copy(bf16[1,128,672]{1,2,0:T(8,128)(2,1)} %bitcast.7) | data formatting | bytes 344064

commit v3 on v2

--- a/solution.py
+++ b/solution.py
@@ -15,6 +15,7 @@
 BF16 = jnp.bfloat16
 STASH, UP, ROWS = 0, 1, 2
 BWD, FWD = 0, 1
+PIECES = 2
 
 
 def nn(left, right):
@@ -62,7 +63,6 @@
     part,
     rs_out,
     rs_in,
-    stat_out,
     stat_in,
     local_sem,
     send_sem,
@@ -173,28 +173,29 @@
         {"pipe": section + 1},
     )
 
+    turn = 1
+
+    def inside_line(*places):
+        conds = [(place >= 0) & (place < groups) for place in places]
+        return functools.reduce(jnp.logical_and, conds)
+
     def gather_from(array, distance, source=None):
-        low, high = z - distance, z + distance
-        if distance:
-            arrive(low >= 0, gathered.at[array, low], gather_sem.at[array, low], {"fsdp": z - 1})
-        send(
-            (low >= 0) & (z < groups - 1),
-            gathered.at[array, low] if source is None else source,
-            gathered.at[array, low],
-            gather_sem.at[array, low],
-            {"fsdp": z + 1},
-        )
-        if distance:
-            arrive(
-                high < groups, gathered.at[array, high], gather_sem.at[array, high], {"fsdp": z + 1}
+        for step in (turn, -turn):
+            at, target = z - step * distance, z + step
+            if distance:
+                arrive(
+                    inside_line(at),
+                    gathered.at[array, at],
+                    gather_sem.at[array, at],
+                    {"fsdp": z - step},
+                )
+            send(
+                inside_line(at, target),
+                gathered.at[array, at] if source is None else source,
+                gathered.at[array, at],
+                gather_sem.at[array, at],
+                {"fsdp": target},
             )
-        send(
-            (high < groups) & (z > 0),
-            gathered.at[array, high] if source is None else source,
-            gathered.at[array, high],
-            gather_sem.at[array, high],
-            {"fsdp": z - 1},
-        )
 
     def whole_rows(array):
         return gathered[array].reshape(groups * share, length)
@@ -310,43 +311,44 @@
         return expo / jnp.sum(expo, axis=-1, keepdims=True)
 
     def scatter_from(which, distance):
-        high, low = z + distance, z - distance
-        for side, at, cond, more, target in (
-            (0, high, high < groups, z > 0, {"fsdp": z + 1}),
-            (1, low, low >= 0, z < groups - 1, {"fsdp": z - 1}),
-        ):
-
-            arrive(cond & more, rs_in.at[which, side, at], rs_sem.at[which, side, at], target)
-
-            def added(side=side, at=at):
-                rs_out[which, side, at] = (
-                    part[which, at] + rs_in[which, side, at].astype(F32)
-                ).astype(BF16)
-
-            def alone(side=side, at=at):
-                rs_out[which, side, at] = part[which, at].astype(BF16)
-
-            when(cond & more, added)
-            when(cond & jnp.logical_not(more), alone)
-            send(
-                cond,
-                rs_out.at[which, side, at],
-                rs_in.at[which, side, at],
-                rs_sem.at[which, side, at],
-                target,
-            )
+        for piece in range(PIECES):
+            rows = pl.ds(piece * (share // PIECES), share // PIECES)
+            for step in (turn, -turn):
+                side = (1 - step) // 2
+                at = z + step * distance
+                cond, more = inside_line(at), inside_line(z - step)
+                came = rs_in.at[which, side, at, rows]
+                sem = rs_sem.at[which, side, at, piece]
+                arrive(cond & more, came, sem, {"fsdp": z + step})
+
+                def added(side=side, at=at, rows=rows):
+                    rs_out[which, side, at, rows] = (
+                        part[which, at, rows] + rs_in[which, side, at, rows].astype(F32)
+                    ).astype(BF16)
+
+                def alone(side=side, at=at, rows=rows):
+                    rs_out[which, side, at, rows] = part[which, at, rows].astype(BF16)
+
+                when(cond & more, added)
+                when(cond & jnp.logical_not(more), alone)
+                send(cond, rs_out.at[which, side, at, rows], came, sem, {"fsdp": z + step})
 
     def scatter_total(which):
-        for side, more, source in (
-            (0, z > 0, {"fsdp": z - 1}),
-            (1, z < groups - 1, {"fsdp": z + 1}),
-        ):
-            arrive(more, rs_in.at[which, side, z], rs_sem.at[which, side, z], source)
-
-            def add(side=side):
-                part[which, z] = part[which, z] + rs_in[which, side, z].astype(F32)
-
-            when(more, add)
+        for piece in range(PIECES):
+            rows = pl.ds(piece * (share // PIECES), share // PIECES)
+            for side, more, source in (
+                (0, z > 0, {"fsdp": z - 1}),
+                (1, z < groups - 1, {"fsdp": z + 1}),
+            ):
+                came = rs_in.at[which, side, z, rows]
+                arrive(more, came, rs_sem.at[which, side, z, piece], source)
+
+                def add(side=side, rows=rows):
+                    part[which, z, rows] = part[which, z, rows] + rs_in[
+                        which, side, z, rows
+                    ].astype(F32)
+
+                when(more, add)
         return part[which, z]
 
     def split_part(which, values):
@@ -449,10 +451,10 @@
         scatter_from(BWD, d)
     rows = whole_rows(STASH).astype(F32)
     row_part = jnp.sum(rows * gain_columns[...] * d_norm, axis=0, keepdims=True)
-    stat_out[...] = jnp.broadcast_to(row_part, (8, length))
+    stat_in[z] = jnp.broadcast_to(row_part, (8, length))
     for d in range(1, groups):
         for cond, other in ((z + d < groups, z + d), (z - d >= 0, z - d)):
-            send(cond, stat_out, stat_in.at[z], stat_sem.at[z], {"fsdp": other})
+            send(cond, stat_in.at[z], stat_in.at[z], stat_sem.at[z], {"fsdp": other})
 
     project(ROWS, FWD)
     share_pair(FWD)
@@ -468,7 +470,6 @@
         scatter_from(FWD, d)
 
     d_share = scatter_total(BWD)
-    stat_in[z] = stat_out[...]
     for d in range(1, groups):
         for cond, other in ((z + d < groups, z + d), (z - d >= 0, z - d)):
             arrive(cond, stat_in.at[other], stat_sem.at[other], {"fsdp": other})
@@ -526,16 +527,15 @@
             pltpu.VMEM((2, groups, share, length), F32),
             pltpu.VMEM((2, 2, groups, share, length), BF16),
             pltpu.VMEM((2, 2, groups, share, length), BF16),
-            pltpu.VMEM((8, length), F32),
             pltpu.VMEM((groups, 8, length), F32),
             dma((7,)),
-            dma((20 * groups + 12 * (reach + 1),)),
+            dma(((12 + 4 * PIECES) * groups + 12 * (reach + 1),)),
             dma((3, groups)),
             dma((2,)),
             dma((2, slots)),
             dma((reach + 1,)),
             dma((max(reach, 1),)),
-            dma((2, 2, groups)),
+            dma((2, 2, groups, PIECES)),
             dma((groups,)),
         ],
         compiler_params=pltpu.CompilerParams(

time: 82.9 us -> 80.7 us (0.973); the launches traced: 82.7 us -> 79.6 us
  Pallas kernels: 78.8 us -> 75.7 us
    pallas_call x1, Pallas kernels: 78.8 us -> 75.7 us  [per_device(): return tuple((jnp.swapaxes(out, 1, 2) for out in call(*args)))]
where the time goes in v3:
time: 80.7 us; the launch traced here: 79.6 us
  Pallas kernels  75.7 us (94%)
  local copies, waits for them, and re-layouts  3.2 us (4%)
    pallas_call x1, Pallas kernels, per_device(): return tuple((jnp.swapaxes(out, 1, 2) for out in call(*args)))  75.7 us
    unnamed x2, local copies, waits for them, and re-layouts  3.2 us

profile of v3, /device:TPU:13, one launch (start us, length us, event | category | flops | bytes accessed | tf_op | source)
XLA Modules:
  0.0 79.6 jit_solution(239331495103351419)
XLA Ops:
  0.6 75.7 %shard_map.131 = (bf16[1,672,128]{2,1,0:T(8,128)(2,1)}, bf16[1,672,128]{2,1,0:T(8,128)(2,1)}) custom-call(bf16[672,128]{1,0:T(8,128)(2,1)} %bitcast.9, bf16[1,672,128]{2,1,0:T(8,128)(2,1)} %bitcast.10, bf16[1,672,128]{2,1,0:T(8,128)(2,1)} %bitcast.11, bf16[1,672,128]{2,1,0:T(8,128)(2,1)} %bitcast.12, bf16[672,128]{1,0:T(8,128)(2,1)} %bitcast.13, ...), custom_call_target="tpu_custom_call" | custom-call | flops 4000000000 | bytes 10000000 | tf_op jit(solution)/shard_map/pallas_call | solution.py:548
  76.4 1.6 %copy.16 = bf16[1,128,672]{1,2,0:T(8,128)(2,1)} copy(bf16[1,128,672]{1,2,0:T(8,128)(2,1)} %bitcast.8) | data formatting | bytes 344064
  78.0 1.6 %copy.17 = bf16[1,128,672]{1,2,0:T(8,128)(2,1)} copy(bf16[1,128,672]{1,2,0:T(8,128)(2,1)} %bitcast.7) | data formatting | bytes 344064
